TPU v7x, 32 devices: a whole 2x2x4 slice. The times are simulated.
32 devices in a mesh: leaf: 16 (over z, x, core), seq: 2 (over y).
Axes of the slice: x: 2, y: 2, z: 4, core: 2. Of those that a mesh axis runs over, the one named last changes fastest.
Arguments:
- queries: bfloat16 [16, 128, 8192], P('leaf', 'seq'), may hold values from -120 to 120
- leaf_kv: bfloat16 [16, 128, 2048], P('leaf', 'seq'), may hold values from -144 to 144
- cache: bfloat16 [2048, 2048], P(('leaf', 'seq')), may hold values from -144 to 144
- out_weight: bfloat16 [8192, 5120], P(None, 'seq'), may hold values from -0.0625 to 0.0625
- parent: int32 [26], replicated, may hold values from 0 to 9, as said below
- owner: int32 [10], replicated, may hold values from 0 to 15, as said below
- lengths: int32 [10], replicated, may hold values from 32 to 128, as said below
Outputs:
- projected: bfloat16 [16, 128, 5120], P('leaf', None, 'seq')
Inputs may be any that keep to these rules, and one draw needn't show every extreme that they name: Entries 0 to 9 are segments: segment i < 4 has parent i - 1 (segment 0 has 0), the next 2 have parent 4 - 1, the next 4 each a segment of those 2; entries 10 on are the leaves, each with a parent among the last 4 segments. `owner`: distinct slots. `lengths`: some segment has exactly 128.
All inputs are finite; a program needn't handle non-finite values.
Results may differ from a plain program's by a relative error of at most 0.012.
Values may be sent and summed in bfloat16 or wider, within the bound.
A program may use at most 256 MiB of HBM per device.

v0:
```python
import math

import jax
import jax.numpy as jnp
from jax import lax
from jax.sharding import PartitionSpec as P

KVH = 8
GROUP = 8
HD = 128
CAP = 128
DEPTH = 6


def branch(parent, leaf_index, seg_count):
    segment = parent[seg_count + leaf_index]
    ancestry = [segment]
    for level in range(DEPTH - 1):
        segment = parent[segment]
        ancestry.append(segment)
    return jnp.stack(ancestry)


def update(carry_state, query_rows, key_value, usable):
    running_max, running_sum, weighted = carry_state
    kv_heads = query_rows.shape[1]
    head_size = query_rows.shape[3]
    width = kv_heads * head_size
    keys = key_value[:, :width].reshape(-1, kv_heads, head_size)
    values = key_value[:, width:].reshape(-1, kv_heads, head_size)
    scores = jnp.einsum("thgd,khd->thgk", query_rows, keys, preferred_element_type=jnp.float32)
    scores = scores * (1.0 / math.sqrt(head_size))
    usable_four = usable[:, None, None, :]
    scores = jnp.where(usable_four, scores, -1e30)
    new_max = jnp.maximum(running_max, jnp.max(scores, axis=3))
    factor = jnp.exp(running_max - new_max)
    expon = jnp.where(usable_four, jnp.exp(scores - new_max[:, :, :, None]), 0.0)
    running_sum = running_sum * factor + jnp.sum(expon, axis=3)
    weights = expon.astype(jnp.bfloat16)
    weighted = weighted * factor[:, :, :, None] + jnp.einsum(
        "thgk,khd->thgd", weights, values, preferred_element_type=jnp.float32
    )
    return (new_max, running_sum, weighted)


def per_device(queries, leaf_kv, cache, out_weight, parent, owner, lengths):
    tokens = queries.shape[1]
    leaf_index = lax.axis_index("leaf")
    seq_index = lax.axis_index("seq")
    ancestry = branch(parent, leaf_index, owner.shape[0])
    owner_slots = owner[ancestry]
    limits = lengths[ancestry]
    query_rows = queries[0].reshape(tokens, KVH, GROUP, HD)
    initial = (
        jnp.full((tokens, KVH, GROUP), -1e30, jnp.float32),
        jnp.zeros((tokens, KVH, GROUP), jnp.float32),
        jnp.zeros((tokens, KVH, GROUP, HD), jnp.float32),
    )
    block_rows = lax.all_gather(cache, ("leaf", "seq"), axis=0, tiled=True)
    row_index = jnp.arange(block_rows.shape[0])
    slot_index = row_index // CAP
    offset = row_index % CAP
    matched = slot_index[:, None] == owner_slots[None, :]
    row_limit = jnp.sum(jnp.where(matched, limits[None, :], 0), axis=1)
    usable = offset < row_limit
    carry_state = lax.cond(
        jnp.any(usable),
        lambda inner: update(inner, query_rows, block_rows, usable[None, :]),
        lambda inner: inner,
        initial,
    )
    position = seq_index * tokens + jnp.arange(tokens)
    fold_block_rows = lax.all_gather(leaf_kv[0], "seq", axis=0, tiled=True)
    key_pos = jnp.arange(fold_block_rows.shape[0])
    fold_usable = key_pos[None, :] <= position[:, None]
    carry_state = lax.cond(
        jnp.int32(0) <= position[-1],
        lambda inner: update(inner, query_rows, fold_block_rows, fold_usable),
        lambda inner: inner,
        carry_state,
    )
    running_max, running_sum, weighted = carry_state
    attended = (weighted / running_sum[:, :, :, None]).astype(jnp.bfloat16).reshape(tokens, -1)
    projected = jnp.dot(
        lax.all_gather(attended, "seq", axis=0, tiled=True),
        out_weight,
        preferred_element_type=jnp.float32,
    ).astype(jnp.bfloat16)
    return projected[None]


def solution(mesh):
    in_specs = (
        P("leaf", "seq", None),
        P("leaf", "seq", None),
        P(("leaf", "seq"), None),
        P(None, "seq"),
        P(),
        P(),
        P(),
    )
    out_specs = P("leaf", None, "seq")
    return jax.shard_map(
        per_device, mesh=mesh, in_specs=in_specs, out_specs=out_specs, check_vma=False
    )
```

profile of v0, /device:TPU:0, one launch (start us, length us, event | category | flops | bytes accessed | tf_op | source)
XLA Modules:
  0.0 230.8 jit_solution(3360491413137300516)
XLA Ops:
  6.5 0.0 copy-start
  6.5 0.0 all-gather.4.cloned.1.call-start
  6.5 0.7 all-gather.4.cloned.1.call-update
  7.3 0.0 all-gather.6.cloned.1.call-start
  7.3 1.2 dynamic_slice.18
  10.5 1.3 dynamic_slice.19
  13.6 1.3 dynamic_slice.20
  16.7 1.2 dynamic_slice.21
  19.6 1.3 dynamic_slice.22
  23.0 1.2 dynamic_slice.23
  24.3 3.8 %stack.21 = s32[6,1]{0,1:T(1,128)S(1)} concatenate(s32[1,1]{0,1:T(1,128)} %bitcast.14, s32[1,1]{0,1:T(1,128)} %bitcast.16, s32[1,1]{0,1:T(1,128)} %bitcast.18, s32[1,1]{0,1:T(1,128)} %bitcast.20, s32[1,1]{0,1:T(1,128)} %bitcast.22, s32[1,1]{0,1:T(1,128)} %bitcast.24), dimensions={0} | concatenate | bytes 48 | tf_op jit(solution)/shard_map/stack | solution.py:21
  28.1 0.0 copy-done
  28.1 0.6 gather_fusion
  28.7 1.3 gather_fusion.1
  30.0 1.5 copy.67
  31.5 0.1 select_reduce_fusion
  31.6 0.6 fusion.30
  32.9 0.6 slice.15
  34.2 15.7 %all-gather = bf16[1,128,2048]{2,1,0:T(8,128)(2,1)} all-gather(bf16[1,64,2048]{2,1,0:T(8,128)(2,1)} %param.12), channel_id=2, replica_groups=mesh['leaf'=16,'seq'=2] {'seq'}, dimensions={1}, use_global_device_ids=true | all-gather | bytes 786432 | tf_op jit(solution)/shard_map/all_gather | solution.py:73
  49.8 42.4 %all-gather.4.cloned.1.call-done = bf16[2048,2048]{1,0:T(8,128)(2,1)} async-done(((bf16[64,2048]{1,0:T(8,128)(2,1)}), bf16[2048,2048]{1,0:T(8,128)(2,1)}) %all-gather.4.cloned.1.call-update) | async-done | bytes 8388624 | tf_op jit(solution)/shard_map/all_gather | solution.py:59
  92.2 63.7 %conditional.2 = (f32[64,8,8]{0,2,1:T(8,128)}, f32[64,8,8]{0,2,1:T(8,128)S(1)}, f32[64,8,8,128]{3,0,2,1:T(8,128)S(1)}) conditional(s32[]{:T(128)} %convert_element_type.23, () %tuple.20, (pred[2048]{0:T(1024)(128)(4,1)S(1)}, bf16[2048,2048]{1,0:T(8,128)(2,1)}, bf16[64,8,8,128]{3,2,1,0:T(8,128)(2,1)S(1)}) %tuple.48), branch_computations={%region_2.3_spmd, %region_3.6_spmd} | conditional | flops 4404559872 | bytes 145938464 | solution.py:66
  92.2 12.3 %copy.47 = bf16[2048,2048]{0,1:T(8,128)(2,1)} copy(bf16[2048,2048]{1,0:T(8,128)(2,1)} %get-tuple-element.82) | data formatting | bytes 16777216 | tf_op jit(solution)/shard_map
  104.5 5.3 %fusion.32 = (bf16[2048,1024]{0,1:T(8,128)(2,1)}, bf16[2048,1024]{0,1:T(8,128)(2,1)S(1)}) fusion(bf16[2048,2048]{0,1:T(8,128)(2,1)} %copy.47), kind=kLoop, calls=%fused_computation.56 | loop fusion | bytes 16777216 | tf_op jit(solution)/shard_map/cond/branch_1_fun/slice | solution.py:30
  109.8 13.6 %bitcast_reduce_fusion = (f32[64,8,8]{0,2,1:T(8,128)S(1)}, f32[8,2048,64,8]{1,2,3,0:T(8,128)}) fusion(pred[2048]{0:T(1024)(128)(4,1)S(1)} %get-tuple-element.36, bf16[2048,8,128,1]{0,2,3,1:T(8,128)(2,1)S(1)} %bitcast.82, bf16[64,8,8,128]{3,2,1,0:T(8,128)(2,1)S(1)} %get-tuple-element.83), kind=kOutput, calls=%fused_computation.3 | convolution fusion | flops 2172645376 | bytes 38815744 | tf_op jit(solution)/shard_map/cond/branch_1_fun/thgd,khd->thgk/dot_general | solution.py:31
  123.4 0.6 exponential_multiply_fusion
  124.0 16.0 %bitcast_add_fusion = f32[64,8,8,128]{3,0,2,1:T(8,128)S(1)} fusion(bf16[2048,8,128,1]{0,2,3,1:T(8,128)(2,1)} %bitcast.87, f32[8,2048,64,8]{1,2,3,0:T(8,128)} %get-tuple-element.103, f32[64,8,8]{0,2,1:T(8,128)} %get-tuple-element.113, pred[2048]{0:T(1024)(128)(4,1)S(1)} %get-tuple-element.36, f32[64,8,8]{0,2,1:T(8,128)S(1)} %get-tuple-element.94), kind=kOutput, calls=%fused_computation.12 | convolution fusion | flops 2189950976 | bytes 39880704 | tf_op jit(solution)/shard_map/cond/branch_1_fun/thgk,khd->thgd/dot_general | solution.py:40
  140.1 15.1 %fusion.3 = f32[64,8,8]{0,2,1:T(8,128)S(1)} fusion(f32[8,2048,64,8]{1,2,3,0:T(8,128)} %get-tuple-element.103, f32[64,8,8]{0,2,1:T(8,128)} %get-tuple-element.113, pred[2048]{0:T(1024)(128)(4,1)S(1)} %get-tuple-element.36), kind=kLoop, calls=%fused_computation.8 | loop fusion | flops 41938944 | bytes 33589248 | tf_op jit(solution)/shard_map/cond/branch_1_fun/reduce_sum | solution.py:38
  155.1 0.8 fusion.15
  155.9 14.7 %conditional.3 = (f32[64,8,8]{0,2,1:T(8,128)S(1)}, f32[64,8,8,128]{3,2,0,1:T(8,128)}) conditional(s32[]{:T(128)} %bitcast.13, (f32[64,8,8]{0,2,1:T(8,128)S(1)}, f32[64,8,8,128]{3,0,2,1:T(8,128)S(1)}) %tuple.22, (s32[]{:T(128)}, s32[64,1]{0,1:T(1,128)S(1)}, s32[64,128]{1,0:T(8,128)S(1)}, bf16[128,2048]{1,0:T(8,128)(2,1)}, ...), branch_computations={%region_6.7_spmd, %region_7.10_spmd} | conditional | flops 274219072 | bytes 14459668 | solution.py:76
  156.2 2.0 copy.50
  158.2 1.8 fusion.33
  160.0 0.1 broadcast_compare_fusion
  160.1 1.1 fusion.16
  161.2 0.8 max.2
  162.0 1.4 fusion.17
  163.3 0.8 multiply_add_fusion
  164.1 0.1 copy.44
  164.2 6.4 %bitcast_add_fusion.1 = f32[64,8,8,128]{3,2,0,1:T(8,128)} fusion(f32[64,8,8,128]{3,0,2,1:T(8,128)S(1)} %get-tuple-element.93, bf16[128,8,128,1]{0,2,3,1:T(8,128)(2,1)} %bitcast.90, bf16[64,8,8,128]{3,0,2,1:T(8,128)(2,1)S(1)} %get-tuple-element.104, f32[64,8,8]{2,0,1:T(8,128)S(1)} %copy.44), kind=kOutput, calls=%fused_computation.21 | convolution fusion | flops 135266304 | bytes 5521408 | tf_op jit(solution)/shard_map/cond/branch_1_fun/thgk,khd->thgd/dot_general | solution.py:40
  170.7 0.1 copy.53
  170.8 2.0 divide_convert_fusion
  172.8 0.3 copy.54
  173.1 1.7 copy.83
  174.8 0.0 all-gather.6.cloned.1.call-update
  174.8 31.9 %all-gather.6.cloned.1.call-done = bf16[128,8192]{1,0:T(8,128)(2,1)} async-done(((bf16[64,8192]{1,0:T(8,128)(2,1)}), bf16[128,8192]{1,0:T(8,128)(2,1)}) %all-gather.6.cloned.1.call-update) | async-done | bytes 2097168 | tf_op jit(solution)/shard_map/all_gather | solution.py:85
  206.7 0.0 copy-start.1
  206.7 17.3 %fusion.22 = bf16[1,128,2560]{2,1,0:T(8,128)(2,1)} fusion(bf16[128,8192]{1,0:T(8,128)(2,1)} %all-gather.6.cloned.1.call-done, bf16[8192,2560]{1,0:T(8,128)(2,1)} %param.14), kind=kOutput, calls=%fused_computation.36 | convolution fusion | flops 5369036800 | bytes 44695552 | tf_op jit(solution)/shard_map/dot_general | solution.py:84
  223.9 0.0 copy-done.1
  (7 shorter events, 0.0 us)
Async XLA Ops:
  6.5 21.5 %copy-start = (s32[10]{0:T(128)S(1)}, s32[10]{0:T(128)}, u32[]{:S(2)}) copy-start(s32[10]{0:T(128)} %param.16) | copy-start | bytes 124
  6.5 85.7 %all-gather.4.cloned.1.call-start = ((), (), s32[]{:S(2)}) async-start(), calls=%async_computation | async-start | bytes 8650752 | tf_op jit(solution)/shard_map/all_gather | solution.py:59
  7.3 199.4 %all-gather.6.cloned.1.call-start = ((), (), s32[]{:S(2)}) async-start(), calls=%async_computation.1 | async-start | bytes 3145728 | tf_op jit(solution)/shard_map/all_gather | solution.py:85
  206.7 17.3 %copy-start.1 = (s32[10]{0:T(128)S(1)}, s32[10]{0:T(128)}, u32[]{:S(2)}) copy-start(s32[10]{0:T(128)} %param.16) | copy-start | bytes 124
Sparse Core Ops, SparseCore 0:
  10.5 81.7 all-gather.3
  174.9 31.6 all-gather.5
where the time goes:
time: 232 us; the launch traced here: 231 us
  waiting for transfers between devices  75 us (32%)
  matrix products  54.5 us (23%)
  local copies, waits for them, and re-layouts  39 us (17%)
  between operations  24.2 us (10%)
  other arithmetic  22.1 us (10%)
  blocking collectives  15.7 us (7%)
    all_gather x1, waiting for transfers between devices, per_device(): block_rows = lax.all_gather(cache, ('leaf', 'seq'), axis=0, tiled=True)  42.4 us
    all_gather x1, waiting for transfers between devices, per_device(): lax.all_gather(attended, 'seq', axis=0, tiled=True)  31.9 us
    dot_general x2, matrix products, update(): jnp.einsum('thgk,khd->thgd', weights, values, preferred_element_type=jnp....  22.5 us
    dot_general x1, matrix products, per_device(): jnp.dot(lax.all_gather(attended, 'seq', axis=0, tiled=True), out_weight,...  17.3 us
    all_gather x1, blocking collectives, per_device(): fold_block_rows = lax.all_gather(leaf_kv[0], 'seq', axis=0, tiled=True)  15.7 us
    reduce_sum x1, other arithmetic, update(): running_sum = running_sum * factor + jnp.sum(expon, axis=3)  15.1 us
    dot_general x2, matrix products, update(): jnp.einsum('thgd,khd->thgk', query_rows, keys, preferred_element_type=jnp...  14.8 us
    another operation x2, local copies, waits for them, and re-layouts  14.3 us
  transfers between devices with their start and end apart: 2, of which 2 were waited for; matrix products, arithmetic and copies ran while one was open for 7% of the time, Pallas kernels for 0%

commit v1 on v0

v1 whole, which is shorter than its diff:
```python
import functools
import math

import jax
import jax.numpy as jnp
from jax import lax
from jax.experimental import pallas as pl
from jax.experimental.pallas import tpu as pltpu
from jax.sharding import PartitionSpec as P

KVH = 8
GROUP = 8
HD = 128
DEPTH = 6
WSLOTS = 4
NEG = -1e30
MESH = pl.DeviceIdType.MESH


def kernel(
    n_leaf, n_seq, cap,
    q_hbm, leaf_hbm, cache_hbm, w_hbm, parent, owner, lengths,
    out,
    kvb, qb, lb, wb, kcat, vcat, att, acc, bias,
    local_sem, w_sem, y_send, y_recv, ring_send, ring_recv, sib_send, sib_recv,
):
    chips = n_leaf // 2
    half = chips // 2
    tokens = q_hbm.shape[1]
    rows = cache_hbm.shape[0]
    all_tokens = n_seq * tokens
    cols = w_hbm.shape[1]
    me = lax.axis_index("leaf")
    seq = lax.axis_index("seq")
    core = lax.rem(me, 2)
    chip = me // 2
    side = lax.rem(chip, 2)
    level = chip // 2
    pos = level * (1 - side) + (chips - 1 - level) * side

    def slot_at(place, which):
        place = lax.rem(place + 2 * chips, chips)
        far = place // half
        return 2 * (2 * (place * (1 - far) + (chips - 1 - place) * far) + far) + which

    right = slot_at(pos + 1, core)
    left = slot_at(pos - 1, core)
    sibling = 2 * chip + 1 - core
    peers = [lax.rem(seq + d, n_seq) for d in range(1, n_seq)]

    def own(c):
        k_cols = pl.ds(pl.multiple_of(c * HD, HD), HD)
        v_cols = pl.ds(pl.multiple_of((KVH + c) * HD, HD), HD)
        q_cols = pl.ds(pl.multiple_of(c * GROUP * HD, HD), GROUP * HD)
        pairs = (
            (cache_hbm.at[:, k_cols], kvb.at[c, me, seq, 0]),
            (cache_hbm.at[:, v_cols], kvb.at[c, me, seq, 1]),
            (leaf_hbm.at[0, :, k_cols], lb.at[c, seq, 0]),
            (leaf_hbm.at[0, :, v_cols], lb.at[c, seq, 1]),
            (q_hbm.at[0, :, q_cols], qb.at[c, seq]),
        )
        return [
            pltpu.make_async_copy(src, dst, local_sem.at[c, i])
            for i, (src, dst) in enumerate(pairs)
        ]

    def weight(c):
        slot = lax.rem(c, WSLOTS)
        k = GROUP * HD
        return pltpu.make_async_copy(
            w_hbm.at[pl.ds(pl.multiple_of(c * k, k), k), :], wb.at[slot], w_sem.at[slot]
        )

    def remote(ref, send, recv, leaf, s):
        return pltpu.make_async_remote_copy(
            src_ref=ref, dst_ref=ref, send_sem=send, recv_sem=recv,
            device_id=(leaf, s), device_id_type=MESH,
        )

    def across(c, d, kind, at, to):
        ref = (kvb.at[c, me, at], lb.at[c, at], qb.at[c, at])[kind]
        return remote(ref, y_send.at[c, d, kind], y_recv.at[c, d, kind], me, to)

    def across_out(c, d, kind):
        return across(c, d, kind, seq, peers[d])

    def across_in(c, d, kind):
        return across(c, d, kind, lax.rem(seq + n_seq - d - 1, n_seq), peers[d])

    def block(c, slot, step, way):
        if step < half:
            return kvb.at[c, slot]
        return kvb.at[c, slot, pl.ds(way * (n_seq // 2), n_seq // 2)]

    def ring_out(c, step, way):
        place = pos - (step - 1) if way == 0 else pos + (step - 1)
        ref = block(c, slot_at(place, core), step, way)
        i = 2 * (step - 1) + way
        return remote(ref, ring_send.at[c, i], ring_recv.at[c, i], (right, left)[way], seq)

    def ring_in(c, step, way):
        place = pos - step if way == 0 else pos + step
        ref = block(c, slot_at(place, core), step, way)
        i = 2 * (step - 1) + way
        return remote(ref, ring_send.at[c, i], ring_recv.at[c, i], (left, right)[way], seq)

    def share(c, step, way, which):
        place = pos - step if way == 0 else pos + step
        ref = block(c, slot_at(place, which), step, way)
        i = 0 if step == 0 else 1 + 2 * (step - 1) + way
        return remote(ref, sib_send.at[c, i], sib_recv.at[c, i], sibling, seq)

    hops = [(step, way) for step in range(1, half + 1) for way in range(2)]

    @pl.loop(0, KVH)
    def _(c):
        for copy in own(c):
            copy.start()

    for c in range(WSLOTS):
        weight(c).start()

    barrier = pltpu.get_barrier_semaphore()
    partners = [(right, seq), (left, seq), (sibling, seq)] + [(me, p) for p in peers]
    for partner in partners:
        pl.semaphore_signal(barrier, inc=1, device_id=partner, device_id_type=MESH)
    pl.semaphore_wait(barrier, len(partners))

    segment = parent[owner.shape[0] + me]
    slots = []
    for a in range(DEPTH):
        slots.append(owner[segment])
        lane = lax.broadcasted_iota(jnp.int32, (8, cap), 1)
        bias[:, a * cap:(a + 1) * cap] = jnp.where(lane < lengths[segment], 0.0, NEG)
        segment = parent[segment]
    acc[...] = jnp.zeros_like(acc)

    stack = max(1, 256 // all_tokens)
    branch_keys = DEPTH * cap
    factor = math.log2(math.e) / math.sqrt(HD)

    def select(c):
        for j in range(n_seq):
            for part, cat in ((0, kcat), (1, vcat)):
                def pick(s, found):
                    piece = kvb[c, s, j, part]
                    return tuple(
                        lax.select(slots[a] == s, piece, found[a]) for a in range(DEPTH)
                    )
                zero = jnp.zeros((rows, HD), jnp.bfloat16)
                found = lax.fori_loop(0, n_leaf, pick, (zero,) * DEPTH)
                for a in range(DEPTH):
                    cat[a * cap + j * rows:a * cap + (j + 1) * rows, :] = found[a]
                at = branch_keys + j * tokens
                cat[at:at + tokens, :] = lb[c, j, part]

    def attend(c):
        def heads(i, carry):
            parts = []
            for g in range(stack):
                lanes = pl.ds(pl.multiple_of((i * stack + g) * HD, HD), HD)
                for j in range(n_seq):
                    parts.append(qb[c, j, :, lanes])
            q = jnp.concatenate(parts, axis=0)
            dims = (((1,), (1,)), ((), ()))
            scores = lax.dot_general(q, kcat[...], dims, preferred_element_type=jnp.float32)
            seen = scores[:, :branch_keys] + bias[0:1, :]
            count = stack * all_tokens
            row = lax.broadcasted_iota(jnp.int32, (count, all_tokens), 0)
            key = lax.broadcasted_iota(jnp.int32, (count, all_tokens), 1)
            own_keys = jnp.where(key <= lax.rem(row, all_tokens), scores[:, branch_keys:], NEG)
            scores = jnp.concatenate([seen, own_keys], axis=1)
            largest = jnp.max(scores, axis=1, keepdims=True)
            expon = jnp.exp2((scores - largest) * factor)
            total = jnp.sum(expon, axis=1, keepdims=True)
            summed = jnp.dot(
                expon.astype(jnp.bfloat16), vcat[...], preferred_element_type=jnp.float32
            )
            result = (summed / total).astype(jnp.bfloat16)
            for g in range(stack):
                lanes = pl.ds(pl.multiple_of((i * stack + g) * HD, HD), HD)
                att[:, lanes] = result[g * all_tokens:(g + 1) * all_tokens]
            return carry
        lax.fori_loop(0, GROUP // stack, heads, 0)

    tile = math.gcd(cols, 512)

    def project(c):
        slot = lax.rem(c, WSLOTS)
        @pl.loop(0, cols // tile)
        def _(i):
            at = pl.ds(pl.multiple_of(i * tile, tile), tile)
            acc[:, at] += jnp.dot(att[...], wb[slot, :, at], preferred_element_type=jnp.float32)

    last = half + 2

    @pl.loop(0, KVH + last)
    def _(tick):
        def when(offset):
            c = tick - offset
            return c, pl.when((c >= 0) & (c < KVH))

        for step in range(half + 1, 0, -1):
            c, guard = when(step)

            @guard
            def _(c=c, step=step):
                if step == 1:
                    for d in range(n_seq - 1):
                        across_in(c, d, 0).wait_recv()
                    for way in range(2):
                        ring_out(c, 1, way).start()
                    share(c, 0, 0, core).start()
                else:
                    for way in range(2):
                        ring_in(c, step - 1, way).wait_recv()
                        if step <= half:
                            ring_out(c, step, way).start()
                        share(c, step - 1, way, core).start()

        c, guard = when(0)

        @guard
        def _(c=c):
            for copy in own(c):
                copy.wait()
            for kind in range(3):
                for d in range(n_seq - 1):
                    across_out(c, d, kind).start()

        c, guard = when(last)

        @guard
        def _(c=c):
            for step, way in [(0, 0)] + hops:
                share(c, step, way, 1 - core).wait_recv()
            for d in range(n_seq - 1):
                across_in(c, d, 1).wait_recv()
                across_in(c, d, 2).wait_recv()
            select(c)
            attend(c)
            weight(c).wait()
            project(c)

            @pl.when(c + WSLOTS < KVH)
            def _():
                weight(c + WSLOTS).start()

    out[0] = acc[...].astype(out.dtype)

    @pl.loop(0, KVH)
    def _(c):
        for kind in range(3):
            for d in range(n_seq - 1):
                across_out(c, d, kind).wait_send()
        for step, way in hops:
            ring_out(c, step, way).wait_send()
        for step, way in [(0, 0)] + hops:
            share(c, step, way, core).wait_send()


def per_device(n_leaf, n_seq, queries, leaf_kv, cache, out_weight, parent, owner, lengths):
    tokens = queries.shape[1]
    rows = cache.shape[0]
    cap = rows * n_seq
    total = tokens * n_seq
    cols = out_weight.shape[1]
    hops = n_leaf // 2
    hbm = pl.BlockSpec(memory_space=pl.ANY)
    smem = pl.BlockSpec(memory_space=pltpu.SMEM)
    keys = DEPTH * cap + total
    dma = pltpu.SemaphoreType.DMA
    bf16 = jnp.bfloat16
    return pl.pallas_call(
        functools.partial(kernel, n_leaf, n_seq, cap),
        out_shape=jax.ShapeDtypeStruct((1, total, cols), bf16),
        in_specs=[hbm] * 4 + [smem] * 3,
        out_specs=pl.BlockSpec(memory_space=pltpu.VMEM),
        scratch_shapes=[
            pltpu.VMEM((KVH, n_leaf, n_seq, 2, rows, HD), bf16),
            pltpu.VMEM((KVH, n_seq, tokens, GROUP * HD), bf16),
            pltpu.VMEM((KVH, n_seq, 2, tokens, HD), bf16),
            pltpu.VMEM((WSLOTS, GROUP * HD, cols), bf16),
            pltpu.VMEM((keys, HD), bf16),
            pltpu.VMEM((keys, HD), bf16),
            pltpu.VMEM((total, GROUP * HD), bf16),
            pltpu.VMEM((total, cols), jnp.float32),
            pltpu.VMEM((8, DEPTH * cap), jnp.float32),
            dma((KVH, 5)),
            dma((WSLOTS,)),
            dma((KVH, n_seq - 1, 3)),
            dma((KVH, n_seq - 1, 3)),
            dma((KVH, hops)),
            dma((KVH, hops)),
            dma((KVH, hops + 1)),
            dma((KVH, hops + 1)),
        ],
        compiler_params=pltpu.CompilerParams(
            collective_id=0, has_side_effects=True, vmem_limit_bytes=58 * 1024 * 1024
        ),
    )(queries, leaf_kv, cache, out_weight, parent, owner, lengths)


def solution(mesh):
    in_specs = (
        P("leaf", "seq", None),
        P("leaf", "seq", None),
        P(("leaf", "seq"), None),
        P(None, "seq"),
        P(),
        P(),
        P(),
    )
    out_specs = P("leaf", None, "seq")
    return jax.shard_map(
        functools.partial(per_device, mesh.shape["leaf"], mesh.shape["seq"]),
        mesh=mesh, in_specs=in_specs, out_specs=out_specs, check_vma=False,
    )
```

time: 232 us -> 88 us (0.38)
  Pallas kernels: 0 us -> 85.9 us
  waiting for transfers between devices: 75 us -> 0 us
  matrix products: 54.5 us -> 0 us
  local copies, waits for them, and re-layouts: 39 us -> 1.97 us
  between operations: 24.2 us -> 0.01 us
  other arithmetic: 22.1 us -> 0 us
  blocking collectives: 15.7 us -> 0 us
    pallas_call x0 -> x1, Pallas kernels: none -> 85.9 us  [per_device(): pl.pallas_call(functools.partial(kernel, n_leaf, n_seq, cap), out_shape=j...]
    all_gather x2 -> x0, waiting for transfers between devices: 74.3 us -> none  [the longest x1 42.4 us: per_device(): block_rows = lax.all_gather(cache, ('leaf', 'seq'), axis=0, tiled=True)]
    dot_general x5 -> x0, matrix products: 54.5 us -> none  [the longest x2 22.5 us: update(): jnp.einsum('thgk,khd->thgd', weights, values, preferred_element_type=jnp....]
    another operation x3 -> x0, local copies, waits for them, and re-layouts: 18.1 us -> none
    all_gather x1 -> x0, blocking collectives: 15.7 us -> none  [per_device(): fold_block_rows = lax.all_gather(leaf_kv[0], 'seq', axis=0, tiled=True)]
    reduce_sum x2 -> x0, other arithmetic: 15.2 us -> none  [the longest x1 15.1 us: update(): running_sum = running_sum * factor + jnp.sum(expon, axis=3)]
    slice x3 -> x0, local copies, waits for them, and re-layouts: 7.66 us -> none  [the longest x2 7.08 us: update(): values = key_value[:, width:].reshape(-1, kv_heads, head_size)]
    dynamic_slice x6 -> x0, local copies, waits for them, and re-layouts: 7.56 us -> none  [the longest x5 6.32 us: branch(): segment = parent[segment]]
  transfers between devices with their start and end apart: 2 -> 0, of which waited for: 2 -> 0; matrix products, arithmetic and copies ran while one was open for 7% -> 0% of each run, Pallas kernels for 0% -> 0%
where the time goes in v1:
time: 88 us; the launch traced here: 87.8 us
  Pallas kernels  85.9 us (98%)
  local copies, waits for them, and re-layouts  1.97 us (2%)
    pallas_call x1, Pallas kernels, per_device(): pl.pallas_call(functools.partial(kernel, n_leaf, n_seq, cap), out_shape=j...  85.9 us
    unnamed x1, local copies, waits for them, and re-layouts  1.97 us

profile of v1, /device:TPU:0, one launch (start us, length us, event | category | flops | bytes accessed | tf_op | source)
XLA Modules:
  0.0 87.8 jit_solution(13929448254568608034)
XLA Ops:
  0.0 85.9 %shard_map.73 = bf16[1,128,2560]{2,1,0:T(8,128)(2,1)} custom-call(bf16[1,64,8192]{2,1,0:T(8,128)(2,1)} %q_hbm.1, bf16[1,64,2048]{2,1,0:T(8,128)(2,1)} %leaf_hbm.1, bf16[64,2048]{1,0:T(8,128)(2,1)} %cache_hbm.1, bf16[8192,2560]{1,0:T(8,128)(2,1)} %w_hbm.1, s32[26]{0:T(128)} %parent.1, s32[10]{0:T(128)} %owner.1, s32[10]{0:T(128)} %lengths.1), custom_call_target="tpu_custom_call" | custom-call | tf_op jit(solution)/shard_map/pallas_call | solution.py:274
  85.9 2.0 %copy.9 = bf16[1,128,2560]{2,1,0:T(8,128)(2,1)} copy(bf16[1,128,2560]{2,1,0:T(8,128)(2,1)} %shard_map.73) | data formatting | bytes 1310720

commit v2 on v1

v2 whole, which is shorter than its diff:
```python
import functools
import math

import jax
import jax.numpy as jnp
from jax import lax
from jax.experimental import pallas as pl
from jax.experimental.pallas import tpu as pltpu
from jax.sharding import PartitionSpec as P

KVH = 8
GROUP = 8
HD = 128
DEPTH = 6
NEG = -1e30
MESH = pl.DeviceIdType.MESH


def kernel(
    n_leaf, n_seq, cap,
    q_hbm, leaf_hbm, cache_hbm, w_hbm, parent, owner, lengths,
    out,
    kvb, qb, lb, wb, kcat, vcat, att, acc, bias,
    local_sem, w_sem, y_send, y_recv, ring_send, ring_recv, sib_send, sib_recv,
    att_send, att_recv,
):
    chips = n_leaf // 2
    half = chips // 2
    tokens = q_hbm.shape[1]
    rows = cache_hbm.shape[0]
    all_tokens = n_seq * tokens
    cols = w_hbm.shape[1]
    me = lax.axis_index("leaf")
    seq = lax.axis_index("seq")
    core = lax.rem(me, 2)
    chip = me // 2
    side = lax.rem(chip, 2)
    level = chip // 2
    pos = level * (1 - side) + (chips - 1 - level) * side

    def slot_at(place, which):
        place = lax.rem(place + 2 * chips, chips)
        far = place // half
        return 2 * (2 * (place * (1 - far) + (chips - 1 - place) * far) + far) + which

    right = slot_at(pos + 1, core)
    left = slot_at(pos - 1, core)
    sibling = 2 * chip + 1 - core
    peers = [lax.rem(seq + d, n_seq) for d in range(1, n_seq)]

    share_heads = KVH // n_seq
    width = GROUP * HD

    def pieces(c, to):
        head = to * share_heads + c
        k_cols = pl.ds(pl.multiple_of(head * HD, HD), HD)
        v_cols = pl.ds(pl.multiple_of((KVH + head) * HD, HD), HD)
        q_cols = pl.ds(pl.multiple_of(head * width, width), width)
        return (
            cache_hbm.at[:, k_cols],
            cache_hbm.at[:, v_cols],
            leaf_hbm.at[0, :, k_cols],
            leaf_hbm.at[0, :, v_cols],
            q_hbm.at[0, :, q_cols],
        )

    def places(c, origin):
        return (
            kvb.at[c, me, origin, 0],
            kvb.at[c, me, origin, 1],
            lb.at[c, origin, 0],
            lb.at[c, origin, 1],
            qb.at[c, origin],
        )

    def own(c):
        return [
            pltpu.make_async_copy(src, dst, local_sem.at[c, i])
            for i, (src, dst) in enumerate(zip(pieces(c, seq), places(c, seq)))
        ]

    def weight(head):
        return pltpu.make_async_copy(
            w_hbm.at[pl.ds(pl.multiple_of(head * width, width), width), :],
            wb.at[head],
            w_sem.at[head],
        )

    def copy_to(src, dst, send, recv, leaf, s):
        return pltpu.make_async_remote_copy(
            src_ref=src, dst_ref=dst, send_sem=send, recv_sem=recv,
            device_id=(leaf, s), device_id_type=MESH,
        )

    def remote(ref, send, recv, leaf, s):
        return copy_to(ref, ref, send, recv, leaf, s)

    def source(d):
        return lax.rem(seq + n_seq - d - 1, n_seq)

    def across_out(c, d, kind):
        return copy_to(
            pieces(c, peers[d])[kind], places(c, seq)[kind],
            y_send.at[c, d, kind], y_recv.at[c, d, kind], me, peers[d],
        )

    def across_in(c, d, kind):
        ref = places(c, source(d))[kind]
        return remote(ref, y_send.at[c, d, kind], y_recv.at[c, d, kind], me, source(d))

    def attended(c, i, d, origin, to):
        ref = att.at[origin, c, i]
        return remote(ref, att_send.at[c, i, d], att_recv.at[c, i, d], me, to)

    def block(c, slot, step, way):
        if step < half:
            return kvb.at[c, slot]
        return kvb.at[c, slot, pl.ds(way * (n_seq // 2), n_seq // 2)]

    def ring_out(c, step, way):
        place = pos - (step - 1) if way == 0 else pos + (step - 1)
        ref = block(c, slot_at(place, core), step, way)
        i = 2 * (step - 1) + way
        return remote(ref, ring_send.at[c, i], ring_recv.at[c, i], (right, left)[way], seq)

    def ring_in(c, step, way):
        place = pos - step if way == 0 else pos + step
        ref = block(c, slot_at(place, core), step, way)
        i = 2 * (step - 1) + way
        return remote(ref, ring_send.at[c, i], ring_recv.at[c, i], (left, right)[way], seq)

    def share(c, step, way, which):
        place = pos - step if way == 0 else pos + step
        ref = block(c, slot_at(place, which), step, way)
        i = 0 if step == 0 else 1 + 2 * (step - 1) + way
        return remote(ref, sib_send.at[c, i], sib_recv.at[c, i], sibling, seq)

    hops = [(step, way) for step in range(1, half + 1) for way in range(2)]

    @pl.loop(0, share_heads)
    def _(c):
        for copy in own(c):
            copy.start()

    barrier = pltpu.get_barrier_semaphore()
    partners = [(right, seq), (left, seq), (sibling, seq)] + [(me, p) for p in peers]
    for partner in partners:
        pl.semaphore_signal(barrier, inc=1, device_id=partner, device_id_type=MESH)
    pl.semaphore_wait(barrier, len(partners))

    segment = parent[owner.shape[0] + me]
    slots = []
    for a in range(DEPTH):
        slots.append(owner[segment])
        lane = lax.broadcasted_iota(jnp.int32, (8, cap), 1)
        bias[:, a * cap:(a + 1) * cap] = jnp.where(lane < lengths[segment], 0.0, NEG)
        segment = parent[segment]
    acc[...] = jnp.zeros_like(acc)

    stack = max(1, 256 // all_tokens)
    branch_keys = DEPTH * cap
    factor = math.log2(math.e) / math.sqrt(HD)

    def select(c):
        for j in range(n_seq):
            for part, cat in ((0, kcat), (1, vcat)):
                def pick(s, found):
                    piece = kvb[c, s, j, part]
                    return tuple(
                        lax.select(slots[a] == s, piece, found[a]) for a in range(DEPTH)
                    )
                zero = jnp.zeros((rows, HD), jnp.bfloat16)
                found = lax.fori_loop(0, n_leaf, pick, (zero,) * DEPTH, unroll=4)
                for a in range(DEPTH):
                    cat[a * cap + j * rows:a * cap + (j + 1) * rows, :] = found[a]
                at = branch_keys + j * tokens
                cat[at:at + tokens, :] = lb[c, j, part]

    def stacked(c, first):
        parts = []
        for g in range(stack):
            lanes = pl.ds(pl.multiple_of((first + g) * HD, HD), HD)
            for j in range(n_seq):
                parts.append(qb[c, j, :, lanes])
        q = jnp.concatenate(parts, axis=0)
        dims = (((1,), (1,)), ((), ()))
        scores = lax.dot_general(q, kcat[...], dims, preferred_element_type=jnp.float32)
        seen = scores[:, :branch_keys] + bias[0:1, :]
        count = stack * all_tokens
        row = lax.broadcasted_iota(jnp.int32, (count, all_tokens), 0)
        key = lax.broadcasted_iota(jnp.int32, (count, all_tokens), 1)
        own_keys = jnp.where(key <= lax.rem(row, all_tokens), scores[:, branch_keys:], NEG)
        scores = jnp.concatenate([seen, own_keys], axis=1)
        largest = jnp.max(scores, axis=1, keepdims=True)
        expon = jnp.exp2((scores - largest) * factor)
        total = jnp.sum(expon, axis=1, keepdims=True)
        summed = jnp.dot(
            expon.astype(jnp.bfloat16), vcat[...], preferred_element_type=jnp.float32
        )
        result = (summed / total).astype(jnp.bfloat16)
        return [result[g * all_tokens:(g + 1) * all_tokens] for g in range(stack)]

    parts_per_head = att.shape[2]
    group = GROUP // parts_per_head

    def attend(c):
        @pl.loop(0, parts_per_head)
        def _(i):
            results = []
            for first in range(0, group, stack):
                results += stacked(c, i * group + first)
            att[seq, c, i] = jnp.concatenate(results, axis=1)
            for d in range(n_seq - 1):
                attended(c, i, d, seq, peers[d]).start()

    tile = math.gcd(cols, 512)

    def project(origin, c):
        head = origin * share_heads + c
        weight(head).wait()
        rows_in = jnp.concatenate(
            [att[origin, c, i] for i in range(parts_per_head)], axis=1
        )

        @pl.loop(0, cols // tile)
        def _(i):
            at = pl.ds(pl.multiple_of(i * tile, tile), tile)
            acc[:, at] += jnp.dot(rows_in, wb[head, :, at], preferred_element_type=jnp.float32)

    last = half + 2

    @pl.loop(0, max(KVH, share_heads + last + 1))
    def _(tick):
        def when(offset):
            c = tick - offset
            return c, pl.when((c >= 0) & (c < share_heads))

        for step in range(half + 1, 0, -1):
            c, guard = when(step)

            @guard
            def _(c=c, step=step):
                if step == 1:
                    for copy in own(c):
                        copy.wait()
                    for d in range(n_seq - 1):
                        across_in(c, d, 0).wait_recv()
                        across_in(c, d, 1).wait_recv()
                    for way in range(2):
                        ring_out(c, 1, way).start()
                    share(c, 0, 0, core).start()
                else:
                    for way in range(2):
                        ring_in(c, step - 1, way).wait_recv()
                        if step <= half:
                            ring_out(c, step, way).start()
                        share(c, step - 1, way, core).start()

        c, guard = when(0)

        @guard
        def _(c=c):
            for kind in range(5):
                for d in range(n_seq - 1):
                    across_out(c, d, kind).start()

        @pl.when(tick < KVH)
        def _():
            weight(lax.rem(seq * share_heads + tick, KVH)).start()

        c, guard = when(last)

        @guard
        def _(c=c):
            for step, way in [(0, 0)] + hops:
                share(c, step, way, 1 - core).wait_recv()
            for d in range(n_seq - 1):
                for kind in range(2, 5):
                    across_in(c, d, kind).wait_recv()
            select(c)
            attend(c)
            project(seq, c)

        c, guard = when(last + 1)

        @guard
        def _(c=c):
            for d in range(n_seq - 1):
                for i in range(parts_per_head):
                    attended(c, i, d, source(d), source(d)).wait_recv()
                project(source(d), c)

    out[0] = acc[...].astype(out.dtype)

    @pl.loop(0, share_heads)
    def _(c):
        for d in range(n_seq - 1):
            for kind in range(5):
                across_out(c, d, kind).wait_send()
            for i in range(parts_per_head):
                attended(c, i, d, seq, peers[d]).wait_send()
        for step, way in hops:
            ring_out(c, step, way).wait_send()
        for step, way in [(0, 0)] + hops:
            share(c, step, way, core).wait_send()


def per_device(n_leaf, n_seq, queries, leaf_kv, cache, out_weight, parent, owner, lengths):
    tokens = queries.shape[1]
    rows = cache.shape[0]
    cap = rows * n_seq
    total = tokens * n_seq
    cols = out_weight.shape[1]
    hops = n_leaf // 2
    heads = KVH // n_seq
    group = min(GROUP, 2 * max(1, 256 // total))
    parts = GROUP // group
    hbm = pl.BlockSpec(memory_space=pl.ANY)
    smem = pl.BlockSpec(memory_space=pltpu.SMEM)
    keys = DEPTH * cap + total
    dma = pltpu.SemaphoreType.DMA
    bf16 = jnp.bfloat16
    return pl.pallas_call(
        functools.partial(kernel, n_leaf, n_seq, cap),
        out_shape=jax.ShapeDtypeStruct((1, total, cols), bf16),
        in_specs=[hbm] * 4 + [smem] * 3,
        out_specs=pl.BlockSpec(memory_space=pltpu.VMEM),
        scratch_shapes=[
            pltpu.VMEM((heads, n_leaf, n_seq, 2, rows, HD), bf16),
            pltpu.VMEM((heads, n_seq, tokens, GROUP * HD), bf16),
            pltpu.VMEM((heads, n_seq, 2, tokens, HD), bf16),
            pltpu.VMEM((KVH, GROUP * HD, cols), bf16),
            pltpu.VMEM((keys, HD), bf16),
            pltpu.VMEM((keys, HD), bf16),
            pltpu.VMEM((n_seq, heads, parts, total, group * HD), bf16),
            pltpu.VMEM((total, cols), jnp.float32),
            pltpu.VMEM((8, DEPTH * cap), jnp.float32),
            dma((heads, 5)),
            dma((KVH,)),
            dma((heads, n_seq - 1, 5)),
            dma((heads, n_seq - 1, 5)),
            dma((heads, hops)),
            dma((heads, hops)),
            dma((heads, hops + 1)),
            dma((heads, hops + 1)),
            dma((heads, parts, n_seq - 1)),
            dma((heads, parts, n_seq - 1)),
        ],
        compiler_params=pltpu.CompilerParams(
            collective_id=0, has_side_effects=True, vmem_limit_bytes=58 * 1024 * 1024
        ),
    )(queries, leaf_kv, cache, out_weight, parent, owner, lengths)


def solution(mesh):
    in_specs = (
        P("leaf", "seq", None),
        P("leaf", "seq", None),
        P(("leaf", "seq"), None),
        P(None, "seq"),
        P(),
        P(),
        P(),
    )
    out_specs = P("leaf", None, "seq")
    return jax.shard_map(
        functools.partial(per_device, mesh.shape["leaf"], mesh.shape["seq"]),
        mesh=mesh, in_specs=in_specs, out_specs=out_specs, check_vma=False,
    )
```

time: 88 us -> 63.9 us (0.73)
  Pallas kernels: 85.9 us -> 61.7 us
    pallas_call x1, Pallas kernels: 85.9 us -> 61.7 us  [per_device(): pl.pallas_call(functools.partial(kernel, n_leaf, n_seq, cap), out_shape=j...]
where the time goes in v2:
time: 63.9 us; the launch traced here: 63.7 us
  Pallas kernels  61.7 us (97%)
  local copies, waits for them, and re-layouts  1.97 us (3%)
    pallas_call x1, Pallas kernels, per_device(): pl.pallas_call(functools.partial(kernel, n_leaf, n_seq, cap), out_shape=j...  61.7 us
    unnamed x1, local copies, waits for them, and re-layouts  1.97 us

profile of v2, /device:TPU:0, one launch (start us, length us, event | category | flops | bytes accessed | tf_op | source)
XLA Modules:
  0.0 63.7 jit_solution(5843851101189836468)
XLA Ops:
  0.0 61.7 %shard_map.73 = bf16[1,128,2560]{2,1,0:T(8,128)(2,1)} custom-call(bf16[1,64,8192]{2,1,0:T(8,128)(2,1)} %q_hbm.1, bf16[1,64,2048]{2,1,0:T(8,128)(2,1)} %leaf_hbm.1, bf16[64,2048]{1,0:T(8,128)(2,1)} %cache_hbm.1, bf16[8192,2560]{1,0:T(8,128)(2,1)} %w_hbm.1, s32[26]{0:T(128)} %parent.1, s32[10]{0:T(128)} %owner.1, s32[10]{0:T(128)} %lengths.1), custom_call_target="tpu_custom_call" | custom-call | tf_op jit(solution)/shard_map/pallas_call | solution.py:323
  61.8 2.0 %copy.9 = bf16[1,128,2560]{2,1,0:T(8,128)(2,1)} copy(bf16[1,128,2560]{2,1,0:T(8,128)(2,1)} %shard_map.73) | data formatting | bytes 1310720

commit v3 on v2

--- a/solution.py
+++ b/solution.py
@@ -148,6 +148,12 @@
         pl.semaphore_signal(barrier, inc=1, device_id=partner, device_id_type=MESH)
     pl.semaphore_wait(barrier, len(partners))
 
+    @pl.loop(0, share_heads)
+    def _(c):
+        for d in range(n_seq - 1):
+            across_out(c, d, 0).start()
+            across_out(c, d, 1).start()
+
     segment = parent[owner.shape[0] + me]
     slots = []
     for a in range(DEPTH):
@@ -155,7 +161,6 @@
         lane = lax.broadcasted_iota(jnp.int32, (8, cap), 1)
         bias[:, a * cap:(a + 1) * cap] = jnp.where(lane < lengths[segment], 0.0, NEG)
         segment = parent[segment]
-    acc[...] = jnp.zeros_like(acc)
 
     stack = max(1, 256 // all_tokens)
     branch_keys = DEPTH * cap
@@ -215,21 +220,36 @@
 
     tile = math.gcd(cols, 512)
 
-    def project(origin, c):
+    def rows_of(origin, c):
+        return jnp.concatenate([att[origin, c, i] for i in range(parts_per_head)], axis=1)
+
+    def product(origin, c, at):
         head = origin * share_heads + c
-        weight(head).wait()
-        rows_in = jnp.concatenate(
-            [att[origin, c, i] for i in range(parts_per_head)], axis=1
-        )
+        return jnp.dot(rows_of(origin, c), wb[head, :, at], preferred_element_type=jnp.float32)
+
+    def project_own():
+        for c in range(share_heads):
+            weight(seq * share_heads + c).wait()
 
         @pl.loop(0, cols // tile)
         def _(i):
             at = pl.ds(pl.multiple_of(i * tile, tile), tile)
-            acc[:, at] += jnp.dot(rows_in, wb[head, :, at], preferred_element_type=jnp.float32)
-
-    last = half + 2
-
-    @pl.loop(0, max(KVH, share_heads + last + 1))
+            part = product(seq, 0, at)
+            for c in range(1, share_heads):
+                part += product(seq, c, at)
+            acc[:, at] = part
+
+    def project(origin, c):
+        weight(origin * share_heads + c).wait()
+
+        @pl.loop(0, cols // tile)
+        def _(i):
+            at = pl.ds(pl.multiple_of(i * tile, tile), tile)
+            acc[:, at] += product(origin, c, at)
+
+    last = half + 1
+
+    @pl.loop(0, max(KVH, share_heads + last))
     def _(tick):
         def when(offset):
             c = tick - offset
@@ -260,7 +280,7 @@
 
         @guard
         def _(c=c):
-            for kind in range(5):
+            for kind in range(2, 5):
                 for d in range(n_seq - 1):
                     across_out(c, d, kind).start()
 
@@ -279,16 +299,15 @@
                     across_in(c, d, kind).wait_recv()
             select(c)
             attend(c)
-            project(seq, c)
-
-        c, guard = when(last + 1)
-
-        @guard
-        def _(c=c):
-            for d in range(n_seq - 1):
-                for i in range(parts_per_head):
-                    attended(c, i, d, source(d), source(d)).wait_recv()
-                project(source(d), c)
+
+    project_own()
+
+    @pl.loop(0, share_heads)
+    def _(c):
+        for d in range(n_seq - 1):
+            for i in range(parts_per_head):
+                attended(c, i, d, source(d), source(d)).wait_recv()
+            project(source(d), c)
 
     out[0] = acc[...].astype(out.dtype)
 

time: 63.9 us -> 59.4 us (0.930)
  Pallas kernels: 61.7 us -> 57.2 us
    pallas_call x1, Pallas kernels: 61.7 us -> 57.2 us  [per_device(): pl.pallas_call(functools.partial(kernel, n_leaf, n_seq, cap), out_shape=j...]
where the time goes in v3:
time: 59.4 us; the launch traced here: 59.2 us
  Pallas kernels  57.2 us (96%)
  local copies, waits for them, and re-layouts  1.97 us (3%)
    pallas_call x1, Pallas kernels, per_device(): pl.pallas_call(functools.partial(kernel, n_leaf, n_seq, cap), out_shape=j...  57.2 us
    unnamed x1, local copies, waits for them, and re-layouts  1.97 us

profile of v3, /device:TPU:0, one launch (start us, length us, event | category | flops | bytes accessed | tf_op | source)
XLA Modules:
  0.0 59.2 jit_solution(2262963982755813630)
XLA Ops:
  0.0 57.2 %shard_map.73 = bf16[1,128,2560]{2,1,0:T(8,128)(2,1)} custom-call(bf16[1,64,8192]{2,1,0:T(8,128)(2,1)} %q_hbm.1, bf16[1,64,2048]{2,1,0:T(8,128)(2,1)} %leaf_hbm.1, bf16[64,2048]{1,0:T(8,128)(2,1)} %cache_hbm.1, bf16[8192,2560]{1,0:T(8,128)(2,1)} %w_hbm.1, s32[26]{0:T(128)} %parent.1, s32[10]{0:T(128)} %owner.1, s32[10]{0:T(128)} %lengths.1), custom_call_target="tpu_custom_call" | custom-call | tf_op jit(solution)/shard_map/pallas_call | solution.py:342
  57.2 2.0 %copy.9 = bf16[1,128,2560]{2,1,0:T(8,128)(2,1)} copy(bf16[1,128,2560]{2,1,0:T(8,128)(2,1)} %shard_map.73) | data formatting | bytes 1310720

commit v4 on v3

--- a/solution.py
+++ b/solution.py
@@ -175,7 +175,7 @@
                         lax.select(slots[a] == s, piece, found[a]) for a in range(DEPTH)
                     )
                 zero = jnp.zeros((rows, HD), jnp.bfloat16)
-                found = lax.fori_loop(0, n_leaf, pick, (zero,) * DEPTH, unroll=4)
+                found = lax.fori_loop(0, n_leaf, pick, (zero,) * DEPTH, unroll=8)
                 for a in range(DEPTH):
                     cat[a * cap + j * rows:a * cap + (j + 1) * rows, :] = found[a]
                 at = branch_keys + j * tokens
@@ -184,7 +184,7 @@
     def stacked(c, first):
         parts = []
         for g in range(stack):
-            lanes = pl.ds(pl.multiple_of((first + g) * HD, HD), HD)
+            lanes = slice((first + g) * HD, (first + g + 1) * HD)
             for j in range(n_seq):
                 parts.append(qb[c, j, :, lanes])
         q = jnp.concatenate(parts, axis=0)
@@ -209,8 +209,7 @@
     group = GROUP // parts_per_head
 
     def attend(c):
-        @pl.loop(0, parts_per_head)
-        def _(i):
+        for i in range(parts_per_head):
             results = []
             for first in range(0, group, stack):
                 results += stacked(c, i * group + first)

time: 59.4 us -> 59.4 us (level)
  no operation moved by 1% of the time
where the time goes in v4:
time: 59.4 us; the launch traced here: 59.2 us
  Pallas kernels  57.2 us (96%)
  local copies, waits for them, and re-layouts  1.97 us (3%)
    pallas_call x1, Pallas kernels, per_device(): pl.pallas_call(functools.partial(kernel, n_leaf, n_seq, cap), out_shape=j...  57.2 us
    unnamed x1, local copies, waits for them, and re-layouts  1.97 us

profile of v4, /device:TPU:0, one launch (start us, length us, event | category | flops | bytes accessed | tf_op | source)
XLA Modules:
  0.0 59.2 jit_solution(11897110681185579472)
XLA Ops:
  0.0 57.2 %shard_map.73 = bf16[1,128,2560]{2,1,0:T(8,128)(2,1)} custom-call(bf16[1,64,8192]{2,1,0:T(8,128)(2,1)} %q_hbm.1, bf16[1,64,2048]{2,1,0:T(8,128)(2,1)} %leaf_hbm.1, bf16[64,2048]{1,0:T(8,128)(2,1)} %cache_hbm.1, bf16[8192,2560]{1,0:T(8,128)(2,1)} %w_hbm.1, s32[26]{0:T(128)} %parent.1, s32[10]{0:T(128)} %owner.1, s32[10]{0:T(128)} %lengths.1), custom_call_target="tpu_custom_call" | custom-call | tf_op jit(solution)/shard_map/pallas_call | solution.py:341
  57.2 2.0 %copy.9 = bf16[1,128,2560]{2,1,0:T(8,128)(2,1)} copy(bf16[1,128,2560]{2,1,0:T(8,128)(2,1)} %shard_map.73) | data formatting | bytes 1310720
